TPU v7x, 256 devices: a whole 4x4x8 slice. The times are simulated.
256 devices in a mesh: row: 8 (over x, core), col: 32 (over y, z).
Axes of the slice: x: 4, y: 4, z: 8, core: 2. Of those that a mesh axis runs over, the one named last changes fastest.
Arguments:
- features: bfloat16 [65536, 256], P(('row', 'col'))
- weight_self: bfloat16 [256, 256], replicated, may hold values from -0.375 to 0.375
- weight_neigh: bfloat16 [256, 256], replicated, may hold values from -0.375 to 0.375
- norm_gain: float32 [256], replicated, may hold values from 0.1 to 1.9
- norm_shift: float32 [256], replicated, may hold values from -3 to 3
- upstream: bfloat16 [65536, 256], P(('row', 'col')), may hold values from -6 to 6
- source_index: int32 [8, 32, 32, 256], P('row', 'col'), may hold values from 0 to 2047
- target_index: int32 [8, 32, 32, 256], P('row', 'col'), may hold values from 0 to 255
- edge_weight: bfloat16 [8, 32, 32, 256], P('row', 'col'), may hold values from 0.029907227 to 0.29882812
- edge_count: int32 [8, 32, 32], P('row', 'col'), may hold values from 0 to 256, as said below
Outputs:
- grad_x: bfloat16 [65536, 256], P(('row', 'col'))
- grad_w_self: float32 [256, 256], replicated
- grad_w_neigh: float32 [256, 256], replicated
- grad_gain: float32 [256], replicated
- grad_shift: float32 [256], replicated
Inputs may be any that keep to these rules, and one draw needn't show every extreme that they name: `edge_count`: some tile and block have exactly 256 live slots; whole tiles may be empty.
All inputs are finite; a program needn't handle non-finite values.
Results may differ from a plain program's by a relative error of at most 0.0057.
Values may be sent and summed in bfloat16 or wider, within the bound.
No kernel may reach another device: no remote copies, remote signals or barrier semaphores. Data moves between devices by JAX's collectives and lax.ppermute only.
A program may use at most 64 MiB of HBM per device.

v0:
```python
import math

import jax
import jax.numpy as jnp
from jax import lax
from jax.sharding import PartitionSpec as P

EPSILON = 1e-05


def body(
    features,
    weight_self,
    weight_neigh,
    norm_gain,
    norm_shift,
    upstream,
    source_index,
    target_index,
    edge_weight,
    edge_count,
):
    node_dev = features.shape[0]
    width = features.shape[1]
    grid_rows = lax.axis_size("row")
    grid_cols = lax.axis_size("col")
    node_total = node_dev * grid_rows * grid_cols
    root = math.sqrt(node_total)
    source_local = source_index[0, 0]
    target_local = target_index[0, 0]
    counts = edge_count[0, 0]
    capacity = source_local.shape[1]
    slot_ids = lax.broadcasted_iota(jnp.int32, (grid_cols, capacity), 1)
    slot_live = slot_ids < counts[:, None]
    weights = jnp.where(slot_live, edge_weight[0, 0], jnp.zeros((), jnp.bfloat16))
    block_ids = lax.broadcasted_iota(jnp.int32, (grid_cols, capacity), 0)
    target_rows = (block_ids * node_dev + target_local).reshape(-1)
    source_rows = source_local.reshape(-1)
    weight_flat = weights.reshape(-1, 1).astype(jnp.float32)
    gathered = lax.all_gather(features, "row", axis=0, tiled=True)
    picked = gathered[source_rows]
    contrib = picked.astype(jnp.float32) * weight_flat
    partial_value = (
        jnp.zeros((grid_cols * node_dev, width), jnp.float32).at[target_rows].add(contrib)
    )
    aggregate = lax.psum_scatter(partial_value, "col", scatter_dimension=0, tiled=True)
    mixed = aggregate.astype(jnp.bfloat16)
    hidden = jnp.dot(features, weight_self, preferred_element_type=jnp.float32) + jnp.dot(
        mixed, weight_neigh, preferred_element_type=jnp.float32
    )
    col_mean = lax.psum(jnp.sum(hidden, axis=0), ("row", "col")) / node_total
    centered = hidden - col_mean
    col_var = lax.psum(jnp.sum(centered * centered, axis=0), ("row", "col")) / node_total
    inv_std = lax.rsqrt(col_var + EPSILON)
    normed = (hidden - col_mean) * inv_std
    scaled = norm_gain * normed + norm_shift
    sigmoid = jax.nn.sigmoid(scaled)
    grad_z = upstream.astype(jnp.float32) * sigmoid * (1.0 + scaled * (1.0 - sigmoid))
    sum_z, sum_zn = lax.psum(
        (jnp.sum(grad_z, axis=0), jnp.sum(grad_z * normed, axis=0)), ("row", "col")
    )
    grad_shift = sum_z / root
    grad_gain = sum_zn / root
    grad_h = (
        norm_gain * inv_std * (grad_z - sum_z / node_total - normed * (sum_zn / node_total))
    ).astype(jnp.bfloat16)
    term_self = jnp.einsum("nf,ng->fg", features, grad_h, preferred_element_type=jnp.float32)
    term_neigh = jnp.einsum("nf,ng->fg", mixed, grad_h, preferred_element_type=jnp.float32)
    sum_self, sum_neigh = lax.psum((term_self, term_neigh), ("row", "col"))
    grad_w_self = sum_self / root
    grad_w_neigh = sum_neigh / root
    grad_m = jnp.einsum(
        "ng,fg->nf", grad_h, weight_neigh, preferred_element_type=jnp.float32
    ).astype(jnp.bfloat16)
    grad_rows = lax.all_gather(grad_m, "col", axis=0, tiled=True)
    back_contrib = grad_rows[target_rows].astype(jnp.float32) * weight_flat
    back_partial = (
        jnp.zeros((grid_rows * node_dev, width), jnp.float32).at[source_rows].add(back_contrib)
    )
    back = lax.psum_scatter(back_partial, "row", scatter_dimension=0, tiled=True)
    own_term = jnp.einsum("ng,fg->nf", grad_h, weight_self, preferred_element_type=jnp.float32)
    grad_x = (own_term + back).astype(jnp.bfloat16)
    return (grad_x, grad_w_self, grad_w_neigh, grad_gain, grad_shift)


def solution(mesh):
    placed = (
        P(("row", "col"), None),
        P(),
        P(),
        P(),
        P(),
        P(("row", "col"), None),
        P("row", "col", None, None),
        P("row", "col", None, None),
        P("row", "col", None, None),
        P("row", "col", None),
    )
    return jax.shard_map(
        body,
        mesh=mesh,
        in_specs=placed,
        out_specs=(P(("row", "col"), None), P(), P(), P(), P()),
        check_vma=False,
    )
```

profile of v0, /device:TPU:8, one launch (start us, length us, event | category | flops | bytes accessed | tf_op | source)
XLA Modules:
  0.0 976.3 jit_solution(16129548522233569952)
XLA Ops:
  7.2 0.7 all-gather.3.cloned.1.call-update
  8.0 0.8 copy.21
  8.8 0.7 copy.22
  9.6 0.7 iota_compare_fusion
  10.3 0.1 broadcast_bitcast_fusion
  10.4 0.8 copy.20
  11.2 0.1 compare_select_fusion.1
  11.3 27.4 %all-gather.3.cloned.1.call-done = bf16[2048,256]{1,0:T(8,128)(2,1)} async-done(((bf16[256,256]{1,0:T(8,128)(2,1)}), bf16[2048,256]{1,0:T(8,128)(2,1)}) %all-gather.3.cloned.1.call-update) | async-done | bytes 1048592 | tf_op jit(solution)/shard_map/all_gather | solution.py:40
  38.7 103.0 %scatter_custom_fusion = f32[8192,256]{1,0:T(8,128)} fusion(s32[8192]{0:T(1024)S(1)} %bitcast.30, f32[8192]{0:T(1024)S(1)} %select_convert_fusion, f32[]{:T(128)} %constant.10.clone.1, bf16[2048,256]{1,0:T(8,128)(2,1)} %all-gather.3.cloned.1.call-done, s32[8192]{0:T(1024)S(1)} %broadcast_clamp_fusion.1), kind=kCustom, calls=%fused_computation.7 | custom fusion | flops 6291456 | bytes 9502724 | tf_op jit(solution)/shard_map/scatter-add | solution.py:44
  141.8 0.2 fusion.19
  142.0 227.9 %reduce-scatter.3.cloned.1.call-done = f32[256,256]{1,0:T(8,128)} async-done(((f32[8192,256]{1,0:T(8,128)}), f32[256,256]{1,0:T(8,128)}) %reduce-scatter.3.cloned.1.call-update) | async-done | bytes 262160 | tf_op jit(solution)/shard_map/reduce_scatter | solution.py:46
  369.9 1.2 fusion.18
  371.1 74.4 %psum.42 = f32[256]{0:T(256)S(1)} all-reduce(f32[256]{0:T(256)S(1)} %get-tuple-element.22), channel_id=1, replica_groups=mesh['row'=8,'col'=32] {'row','col'}, use_global_device_ids=true, to_apply=%region_3.4 | all-reduce | flops 256 | bytes 2048 | tf_op jit(solution)/shard_map/psum | solution.py:51
  445.5 0.1 multiply_reduce_fusion.1
  445.5 73.5 %psum.43 = f32[256]{0:T(256)S(1)} all-reduce(f32[256]{0:T(256)S(1)} %multiply_reduce_fusion.1), channel_id=1, replica_groups=mesh['row'=8,'col'=32] {'row','col'}, use_global_device_ids=true, to_apply=%region_5.6 | all-reduce | flops 256 | bytes 2048 | tf_op jit(solution)/shard_map/psum | solution.py:53
  519.1 0.2 fusion.17
  519.2 74.1 %all-reduce = (f32[256]{0:T(256)S(1)}, f32[256]{0:T(256)S(1)}) all-reduce(f32[256]{0:T(256)S(1)} %get-tuple-element.11, f32[256]{0:T(256)S(1)} %get-tuple-element.10), channel_id=1, replica_groups=mesh['row'=8,'col'=32] {'row','col'}, use_global_device_ids=true, to_apply=%region_9.10 | all-reduce | flops 512 | bytes 4096 | tf_op jit(solution)/shard_map/psum | solution.py:59
  593.3 0.6 broadcast_multiply_fusion.2
  593.9 0.2 multiply_convert_fusion
  594.1 0.9 convolution_convert_fusion
  595.0 0.9 convolution_bitcast_fusion
  595.9 1.9 fusion.11
  597.8 0.2 reduce-scatter.5.cloned.1.call-start
  598.1 74.3 %all-gather.5.cloned.1.call-done = bf16[8192,256]{1,0:T(8,128)(2,1)} async-done(((bf16[256,256]{1,0:T(8,128)(2,1)}), bf16[8192,256]{1,0:T(8,128)(2,1)}) %all-gather.5.cloned.1.call-update) | async-done | bytes 4194320 | tf_op jit(solution)/shard_map/all_gather | solution.py:75
  672.4 101.3 %scatter_custom_fusion.1 = f32[2048,256]{1,0:T(8,128)} fusion(s32[8192]{0:T(1024)S(1)} %bitcast.35, f32[8192]{0:T(1024)S(1)} %select_convert_fusion, f32[]{:T(128)} %constant.10.clone.1, bf16[8192,256]{1,0:T(8,128)(2,1)} %all-gather.5.cloned.1.call-done, s32[8192]{0:T(1024)S(1)} %broadcast_clamp_fusion), kind=kCustom, calls=%fused_computation.4 | custom fusion | flops 6291456 | bytes 6356996 | tf_op jit(solution)/shard_map/scatter-add | solution.py:78
  773.7 156.7 %all-reduce.4.cloned.1.call-done = (f32[256,256]{0,1:T(8,128)}, f32[256,256]{0,1:T(8,128)}) async-done(((f32[256,256]{0,1:T(8,128)}, f32[256,256]{0,1:T(8,128)}), (f32[256,256]{0,1:T(8,128)}, f32[256,256]{0,1:T(8,128)})) %all-reduce.4.cloned.1.call-update) | async-done | bytes 524304 | tf_op jit(solution)/shard_map/psum | solution.py:69
  930.4 1.0 broadcast_multiply_fusion.1
  931.4 0.8 copy.16
  932.3 1.0 broadcast_multiply_fusion
  933.2 0.8 copy.17
  934.1 33.8 %reduce-scatter.5.cloned.1.call-done = f32[256,256]{1,0:T(8,128)} async-done(((f32[2048,256]{1,0:T(8,128)}), f32[256,256]{1,0:T(8,128)}) %reduce-scatter.5.cloned.1.call-update) | async-done | bytes 262160 | tf_op jit(solution)/shard_map/reduce_scatter | solution.py:80
  967.9 1.8 fusion.9
  (29 shorter events, 0.4 us)
Async XLA Ops:
  7.2 362.8 %copy-start = (bf16[256,256]{1,0:T(8,128)(2,1)S(1)}, bf16[256,256]{1,0:T(8,128)(2,1)}, u32[]{:S(2)}) copy-start(bf16[256,256]{1,0:T(8,128)(2,1)} %param.12) | copy-start | bytes 393220
  7.2 31.5 %all-gather.3.cloned.1.call-start = ((), (), s32[]{:S(2)}) async-start(), calls=%async_computation.2 | async-start | bytes 1179648 | tf_op jit(solution)/shard_map/all_gather | solution.py:40
  7.9 362.0 %reduce-scatter.3.cloned.1.call-start = ((), (), s32[]{:S(2)}) async-start(), calls=%async_computation.3 | async-start | bytes 8650752 | tf_op jit(solution)/shard_map/reduce_scatter | solution.py:46
  38.7 103.1 %copy-start.1 = (bf16[256,256]{1,0:T(8,128)(2,1)S(1)}, bf16[256,256]{1,0:T(8,128)(2,1)}, u32[]{:S(2)}) copy-start(bf16[256,256]{1,0:T(8,128)(2,1)} %param.10) | copy-start | bytes 393220
  38.7 103.1 %copy-start.3 = (bf16[256,256]{1,0:T(8,128)(2,1)S(1)}, bf16[256,256]{1,0:T(8,128)(2,1)}, u32[]{:S(2)}) copy-start(bf16[256,256]{1,0:T(8,128)(2,1)} %param.11) | copy-start | bytes 393220
  38.7 480.4 %copy-start.4 = (f32[256]{0:T(256)S(1)}, f32[256]{0:T(256)}, u32[]{:S(2)}) copy-start(f32[256]{0:T(256)} %param.13) | copy-start | bytes 3076
  38.7 480.4 %copy-start.2 = (bf16[256,256]{1,0:T(8,128)(2,1)S(1)}, bf16[256,256]{1,0:T(8,128)(2,1)}, u32[]{:S(2)}) copy-start(bf16[256,256]{1,0:T(8,128)(2,1)} %param.15) | copy-start | bytes 393220
  38.7 480.4 %copy-start.5 = (f32[256]{0:T(256)S(1)}, f32[256]{0:T(256)}, u32[]{:S(2)}) copy-start(f32[256]{0:T(256)} %param.14) | copy-start | bytes 3076
  141.8 530.6 %all-gather.5.cloned.1.call-start = ((), (), s32[]{:S(2)}) async-start(), calls=%async_computation.4 | async-start | bytes 4325376 | tf_op jit(solution)/shard_map/all_gather | solution.py:75
  595.0 335.5 %all-reduce.4.cloned.1.call-start = ((), (), s32[]{:S(2)}) async-start(), calls=%async_computation.6 | async-start | bytes 1048576 | tf_op jit(solution)/shard_map/psum | solution.py:69
  597.8 370.1 %reduce-scatter.5.cloned.1.call-start = ((), (), s32[]{:S(2)}) async-start(), calls=%async_computation.5 | async-start | bytes 2359296 | tf_op jit(solution)/shard_map/reduce_scatter | solution.py:80
Sparse Core Ops, SparseCore 0:
  9.9 28.7 all-gather.2
  141.9 228.0 reduce-scatter.2
  595.1 77.2 all-gather.4
  679.4 251.0 all-reduce.3
  933.0 34.8 reduce-scatter.4
where the time goes:
time: 978 us; the launch traced here: 976 us
  waiting for transfers between devices  521 us (53%)
  blocking collectives  222 us (23%)
  other arithmetic  208 us (21%)
  between operations  13.9 us (1%)
    reduce_scatter x1, waiting for transfers between devices, body(): lax.psum_scatter(partial_value, 'col', scatter_dimension=0, tiled=True)  228 us
    psum x1, waiting for transfers between devices, body(): sum_self, sum_neigh = lax.psum((term_self, term_neigh), ('row', 'col'))  157 us
    scatter-add x1, other arithmetic, body(): jnp.zeros((grid_cols * node_dev, width), jnp.float32).at[target_rows]  103 us
    scatter-add x1, other arithmetic, body(): jnp.zeros((grid_rows * node_dev, width), jnp.float32).at[source_rows]  101 us
    psum x1, blocking collectives, body(): col_mean = lax.psum(jnp.sum(hidden, axis=0), ('row', 'col')) / node_total  74.4 us
    all_gather x1, waiting for transfers between devices, body(): grad_rows = lax.all_gather(grad_m, 'col', axis=0, tiled=True)  74.3 us
    psum x1, blocking collectives, body(): lax.psum((jnp.sum(grad_z, axis=0), jnp.sum(grad_z * normed, axis=0)), ('r...  74.1 us
    psum x1, blocking collectives, body(): lax.psum(jnp.sum(centered * centered, axis=0), ('row', 'col')) / node_total  73.5 us
  transfers between devices with their start and end apart: 5, of which 5 were waited for; matrix products, arithmetic and copies ran while one was open for 11% of the time, Pallas kernels for 0%

commit v1 on v0

v1 whole, which is shorter than its diff:
```python
import math

import jax
import jax.numpy as jnp
from jax import lax
from jax.experimental import pallas as pl
from jax.experimental.pallas import tpu as pltpu
from jax.sharding import Mesh
from jax.sharding import PartitionSpec as P

EPSILON = 1e-05
BF = jnp.bfloat16
F32 = jnp.float32
NX, NC, NY, NZ = 4, 2, 4, 8
ALL = ("x", "c", "y", "z")
BLK = 256
VMEM = pl.BlockSpec(memory_space=pltpu.VMEM)
SMEM = pl.BlockSpec(memory_space=pltpu.SMEM)
PARAMS = pltpu.CompilerParams(vmem_limit_bytes=48 * 2**20)


def iota_bf(shape, dim):
    return lax.broadcasted_iota(jnp.int32, shape, dim).astype(F32).astype(BF)


def one_hot(iota, index, value):
    return jnp.where(iota == index, value, jnp.zeros((), BF))


def forward_kernel(x_ref, edge_ref, out_ref, picked_ref):
    lane = iota_bf((BLK, BLK), 1)
    sub = iota_bf((BLK, BLK), 0)
    one = jnp.ones((), BF)

    def dest(z, carry):
        scatter = []
        for y in range(NY):
            tile = edge_ref[y * NZ + z]
            cols = tile.T
            low = one_hot(lane, cols[:, 0:1].astype(BF), one)
            high = cols[:, 1:2]
            select = jnp.concatenate(
                [low * jnp.where(high == float(h), 1.0, 0.0).astype(BF) for h in range(NX * NC)],
                axis=1,
            )
            rows = x_ref[y * NX * NC : (y + 1) * NX * NC].reshape(NX * NC * BLK, BLK)
            picked = jnp.dot(select, rows, preferred_element_type=F32)
            picked_ref[y * BLK : (y + 1) * BLK] = picked.astype(BF)
            scatter.append(one_hot(sub, tile[2:3].astype(BF), tile[3:4].astype(BF)))
        out = jnp.dot(
            jnp.concatenate(scatter, axis=1), picked_ref[...], preferred_element_type=F32
        )
        out_ref[z] = out.astype(BF)
        return carry

    lax.fori_loop(0, NZ, dest, 0)


def backward_kernel(core_ref, grad_ref, edge_ref, send_ref, keep_ref, picked_ref, weight_ref):
    lane = iota_bf((BLK, BLK), 1)
    sub = iota_bf((BLK, BLK), 0)
    one = jnp.ones((), BF)
    core = core_ref[0].astype(F32)

    def source(y, carry):
        highs = []
        for z in range(NZ):
            tile = edge_ref[y * NZ + z]
            cols = tile.T
            gather = one_hot(lane, cols[:, 2:3].astype(BF), one)
            picked = jnp.dot(gather, grad_ref[z], preferred_element_type=F32)
            picked_ref[z * BLK : (z + 1) * BLK] = picked.astype(BF)
            weight_ref[:, z * BLK : (z + 1) * BLK] = one_hot(
                sub, tile[0:1].astype(BF), tile[3:4].astype(BF)
            )
            highs.append(tile[1:2])
        high = jnp.concatenate(highs, axis=1)
        for x in range(NX):
            for ref, part in ((send_ref, 1.0 - core), (keep_ref, core)):
                mask = jnp.where(high == 2.0 * x + part, 1.0, 0.0).astype(BF)
                out = jnp.dot(
                    weight_ref[...] * mask, picked_ref[...], preferred_element_type=F32
                )
                ref[y * NX + x] = out.astype(ref.dtype)
        return carry

    lax.fori_loop(0, NY, source, 0)


def exchange(value, axes):
    return lax.all_to_all(value, axes, 0, 0, tiled=False)


def everywhere(value, axes, count):
    return exchange(jnp.broadcast_to(value[None], (count,) + value.shape), axes)


def merge(mean, spread, rows):
    total = jnp.mean(mean, axis=0)
    moved = jnp.sum((mean - total) ** 2, axis=0)
    return total, jnp.sum(spread, axis=0) + rows * moved


def silu_parts(hidden, mean, inv_std, gain, shift, upstream):
    normed = (hidden - mean) * inv_std
    scaled = gain * normed + shift
    sigmoid = jax.nn.sigmoid(scaled)
    grad_z = upstream.astype(F32) * sigmoid * (1.0 + scaled * (1.0 - sigmoid))
    return normed, grad_z


def body(
    features,
    weight_self,
    weight_neigh,
    norm_gain,
    norm_shift,
    upstream,
    source_index,
    target_index,
    edge_weight,
    edge_count,
):
    node_total = BLK * NX * NC * NY * NZ
    root = math.sqrt(node_total)
    core = lax.axis_index("c").astype(jnp.int32).reshape(1)

    gathered = lax.all_gather(features, ("y", "x", "c"), axis=0, tiled=False)
    gathered = gathered.reshape(NY * NX * NC, BLK, BLK)
    pair = jnp.stack([features, upstream])
    pair_all = lax.all_gather(pair, "z", axis=0, tiled=False)

    source = source_index[0, 0]
    counts = edge_count[0, 0]
    slot = lax.broadcasted_iota(jnp.int32, source.shape, 1)
    weight = jnp.where(slot < counts[:, None], edge_weight[0, 0], jnp.zeros((), BF))
    edges = jnp.stack(
        [
            (source % BLK).astype(F32).astype(BF),
            (source // BLK).astype(F32).astype(BF),
            target_index[0, 0].astype(F32).astype(BF),
            weight,
        ],
        axis=1,
    )
    edges = exchange(edges.reshape(NY, NZ * 4, BLK), "y").astype(F32)
    edges = edges.reshape(NY * NZ, 4, BLK)
    edges = jnp.concatenate([edges, jnp.zeros_like(edges)], axis=1)

    partial = pl.pallas_call(
        forward_kernel,
        out_shape=jax.ShapeDtypeStruct((NZ, BLK, BLK), BF),
        in_specs=[VMEM, VMEM],
        out_specs=VMEM,
        scratch_shapes=[pltpu.VMEM((NY * BLK, BLK), BF)],
        compiler_params=PARAMS,
        name="forward_edges",
    )(gathered, edges)
    aggregate = jnp.sum(exchange(partial, "z").astype(F32), axis=0)
    mixed = aggregate.astype(BF)
    mixed_all = lax.all_gather(mixed, "z", axis=0, tiled=True)

    hidden = jnp.dot(features, weight_self, preferred_element_type=F32) + jnp.dot(
        mixed, weight_neigh, preferred_element_type=F32
    )
    mean = jnp.mean(hidden, axis=0)
    spread = jnp.sum((hidden - mean) ** 2, axis=0)
    got = everywhere(jnp.stack([mean, spread]), ("x", "c"), NX * NC)
    mean, spread = merge(got[:, 0], got[:, 1], BLK)
    got = everywhere(jnp.stack([mean, spread]), ("y", "z"), NY * NZ)
    col_mean, spread = merge(got[:, 0], got[:, 1], BLK * NX * NC)
    inv_std = lax.rsqrt(spread / node_total + EPSILON)

    normed, grad_z = silu_parts(hidden, col_mean, inv_std, norm_gain, norm_shift, upstream)
    sums = jnp.stack([jnp.sum(grad_z, axis=0), jnp.sum(grad_z * normed, axis=0)])
    sums = jnp.sum(everywhere(sums, ("x", "c"), NX * NC), axis=0)
    sums = jnp.sum(everywhere(sums, ("y", "z"), NY * NZ), axis=0)
    sum_z, sum_zn = sums[0], sums[1]
    grad_shift = sum_z / root
    grad_gain = sum_zn / root

    scale = norm_gain * inv_std
    mean_z, mean_zn = sum_z / node_total, sum_zn / node_total
    grad_h = (scale * (grad_z - mean_z - normed * mean_zn)).astype(BF)

    features_all = pair_all[:, 0].reshape(NZ * BLK, BLK)
    upstream_all = pair_all[:, 1].reshape(NZ * BLK, BLK)
    hidden_all = jnp.dot(features_all, weight_self, preferred_element_type=F32) + jnp.dot(
        mixed_all, weight_neigh, preferred_element_type=F32
    )
    normed_all, grad_z_all = silu_parts(
        hidden_all, col_mean, inv_std, norm_gain, norm_shift, upstream_all
    )
    grad_h_all = (scale * (grad_z_all - mean_z - normed_all * mean_zn)).astype(BF)
    grad_m = jnp.einsum(
        "ng,fg->nf", grad_h_all, weight_neigh, preferred_element_type=F32
    ).astype(BF)

    half = jax.ShapeDtypeStruct((NY * NX, BLK, BLK), BF)
    send, keep = pl.pallas_call(
        backward_kernel,
        out_shape=(half, half),
        in_specs=[SMEM, VMEM, VMEM],
        out_specs=(VMEM, VMEM),
        scratch_shapes=[pltpu.VMEM((NZ * BLK, BLK), BF), pltpu.VMEM((BLK, NZ * BLK), BF)],
        compiler_params=PARAMS,
        name="backward_edges",
    )(core, grad_m.reshape(NZ, BLK, BLK), edges)
    other = lax.ppermute(send, "c", [(0, 1), (1, 0)])
    both = (keep.astype(F32) + other.astype(F32)).astype(BF)
    back = jnp.sum(exchange(both, ("y", "x")).astype(F32), axis=0)
    own_term = jnp.einsum("ng,fg->nf", grad_h, weight_self, preferred_element_type=F32)
    grad_x = (own_term + back).astype(BF)

    inputs = jnp.concatenate([features, mixed], axis=1)
    term = jnp.einsum("nf,ng->fg", inputs, grad_h, preferred_element_type=F32)
    devices = NX * NC * NY * NZ
    term = exchange(term.reshape(devices, 2 * BLK // devices, BLK), ALL)
    term = jnp.sum(term, axis=0) / root
    whole = everywhere(term, ALL, devices).reshape(2 * BLK, BLK)
    return (grad_x, whole[:BLK], whole[BLK:], grad_gain, grad_shift)


def solution(mesh):
    grid = Mesh(mesh.devices.reshape(NX, NC, NY, NZ), ALL)
    row, col = ("x", "c"), ("y", "z")
    placed = (
        P(ALL, None),
        P(),
        P(),
        P(),
        P(),
        P(ALL, None),
        P(row, col, None, None),
        P(row, col, None, None),
        P(row, col, None, None),
        P(row, col, None),
    )
    return jax.shard_map(
        body,
        mesh=grid,
        in_specs=placed,
        out_specs=(P(ALL, None), P(), P(), P(), P()),
        check_vma=False,
    )
```

time: 978 us -> 312 us (0.32)
  waiting for transfers between devices: 521 us -> 155 us
  other arithmetic: 208 us -> 10.1 us
  blocking collectives: 222 us -> 40 us
  starting transfers between devices: 0.38 us -> 40.2 us
  Pallas kernels: 0 us -> 31.2 us
    reduce_scatter x2 -> x0, waiting for transfers between devices: 262 us -> none  [the longest x1 228 us: body(): lax.psum_scatter(partial_value, 'col', scatter_dimension=0, tiled=True)]
    psum x3 -> x0, blocking collectives: 222 us -> none  [the longest x1 74.4 us: body(): col_mean = lax.psum(jnp.sum(hidden, axis=0), ('row', 'col')) / node_total]
    scatter-add x2 -> x0, other arithmetic: 204 us -> none  [the longest x1 103 us: body(): jnp.zeros((grid_cols * node_dev, width), jnp.float32).at[target_rows]]
    psum x1 -> x0, waiting for transfers between devices: 157 us -> none  [body(): sum_self, sum_neigh = lax.psum((term_self, term_neigh), ('row', 'col'))]
    all_to_all x0 -> x7, waiting for transfers between devices: none -> 104 us  [exchange(): return lax.all_to_all(value, axes, 0, 0, tiled=False)]
    all_gather x2 -> x3, waiting for transfers between devices: 102 us -> 50.5 us  [the longest x1 43.6 us: body(): gathered = lax.all_gather(features, ('y', 'x', 'c'), axis=0, tiled=False)]
    all_to_all x0 -> x7, starting transfers between devices: none -> 40.1 us  [exchange(): return lax.all_to_all(value, axes, 0, 0, tiled=False)]
    all_to_all x0 -> x2, blocking collectives: none -> 40 us  [exchange(): return lax.all_to_all(value, axes, 0, 0, tiled=False)]
  transfers between devices with their start and end apart: 5 -> 11, of which waited for: 5 -> 9; matrix products, arithmetic and copies ran while one was open for 11% -> 7% of each run, Pallas kernels for 0% -> 6%
where the time goes in v1:
time: 312 us; the launch traced here: 309 us
  waiting for transfers between devices  155 us (50%)
  starting transfers between devices  40.2 us (13%)
  blocking collectives  40 us (13%)
  Pallas kernels  31.2 us (10%)
  between operations  14.1 us (5%)
  other arithmetic  10.1 us (3%)
  local copies, waits for them, and re-layouts  9.79 us (3%)
  matrix products  8.33 us (3%)
    all_to_all x7, waiting for transfers between devices, exchange(): return lax.all_to_all(value, axes, 0, 0, tiled=False)  104 us
    all_gather x1, waiting for transfers between devices, body(): gathered = lax.all_gather(features, ('y', 'x', 'c'), axis=0, tiled=False)  43.6 us
    all_to_all x7, starting transfers between devices, exchange(): return lax.all_to_all(value, axes, 0, 0, tiled=False)  40.1 us
    all_to_all x2, blocking collectives, exchange(): return lax.all_to_all(value, axes, 0, 0, tiled=False)  40 us
    pallas_call x1, Pallas kernels, body(): pl.pallas_call(forward_kernel, out_shape=jax.ShapeDtypeStruct((NZ, BLK, B...  17.5 us
    pallas_call x1, Pallas kernels, body(): pl.pallas_call(backward_kernel, out_shape=(half, half), in_specs=[SMEM, V...  13.8 us
    all_gather x1, waiting for transfers between devices, body(): mixed_all = lax.all_gather(mixed, 'z', axis=0, tiled=True)  6.89 us
  transfers between devices with their start and end apart: 11, of which 9 were waited for; matrix products, arithmetic and copies ran while one was open for 7% of the time, Pallas kernels for 6%

profile of v1, /device:TPU:8, one launch (start us, length us, event | category | flops | bytes accessed | tf_op | source)
XLA Modules:
  0.0 309.2 jit_solution(3969978069755267769)
XLA Ops:
  7.9 0.8 fusion.27
  11.0 5.4 %all-to-all-start = ((bf16[4,32,256]{2,1,0:T(8,128)(2,1)}), bf16[4,32,256]{2,1,0:T(8,128)(2,1)S(1)}, u32[]{:S(2)}, u32[]{:S(2)}) async-start(bf16[4,32,256]{2,1,0:T(8,128)(2,1)} %reshape.267), calls=%async_computation | async-start | bytes 131072 | tf_op jit(solution)/shard_map/all_to_all | solution.py:91
  16.4 1.7 pad_maximum_fusion
  18.2 2.4 all-to-all-done
  20.7 43.6 %all-gather.8.cloned.1.call-done = bf16[8192,256]{1,0:T(8,128)(2,1)} async-done(((bf16[256,256]{1,0:T(8,128)(2,1)}), bf16[8192,256]{1,0:T(8,128)(2,1)}) %all-gather.8.cloned.1.call-update) | async-done | bytes 4194320 | tf_op jit(solution)/shard_map/all_gather | solution.py:128
  64.2 2.2 copy-done.1
  66.4 17.5 %forward_edges.1 = bf16[8,256,256]{2,1,0:T(8,128)(2,1)} custom-call(bf16[32,256,256]{2,1,0:T(8,128)(2,1)S(1)} %bitcast.74, f32[32,8,256]{2,1,0:T(8,128)S(1)} %pad_convert_fusion.edge_ref), custom_call_target="tpu_custom_call" | custom-call | tf_op jit(solution)/shard_map/forward_edges/pallas_call | solution.py:150
  83.9 7.2 %all-to-all-start.1 = ((bf16[8,256,256]{2,1,0:T(8,128)(2,1)}), bf16[8,256,256]{2,1,0:T(8,128)(2,1)S(1)}, u32[]{:S(2)}, u32[]{:S(2)}) async-start(bf16[8,256,256]{2,1,0:T(8,128)(2,1)} %forward_edges.1), calls=%async_computation.1 | async-start | bytes 2097152 | tf_op jit(solution)/shard_map/all_to_all | solution.py:91
  91.3 35.3 %all-to-all-done.1 = bf16[8,256,256]{2,1,0:T(8,128)(2,1)S(1)} async-done(((bf16[8,256,256]{2,1,0:T(8,128)(2,1)}), bf16[8,256,256]{2,1,0:T(8,128)(2,1)S(1)}, u32[]{:S(2)}, u32[]{:S(2)}) %all-to-all-start.1) | async-done | bytes 1048608 | tf_op jit(solution)/shard_map/all_to_all | solution.py:91
  127.1 9.1 %all_to_all.45 = f32[8,2,256]{2,1,0:T(2,128)S(1)} all-to-all(f32[8,2,256]{2,1,0:T(2,128)S(1)} %broadcast_in_dim.15), channel_id=1, replica_groups=mesh['x'=4,'c'=2,'y'=4,'z'=8] {'x','c'}, dimensions={0} | all-to-all | bytes 32768 | tf_op jit(solution)/shard_map/all_to_all | solution.py:91
  137.0 7.8 %all-to-all-start.3 = ((f32[32,2,256]{2,1,0:T(2,128)}), f32[32,2,256]{2,1,0:T(2,128)S(1)}, u32[]{:S(2)}, u32[]{:S(2)}) async-start(f32[32,2,256]{2,1,0:T(2,128)} %broadcast_in_dim.16), calls=%async_computation.3 | async-start | bytes 131072 | tf_op jit(solution)/shard_map/all_to_all | solution.py:91
  145.6 8.1 %all-to-all-done.3 = f32[32,2,256]{2,1,0:T(2,128)S(1)} async-done(((f32[32,2,256]{2,1,0:T(2,128)}), f32[32,2,256]{2,1,0:T(2,128)S(1)}, u32[]{:S(2)}, u32[]{:S(2)}) %all-to-all-start.3) | async-done | bytes 65568 | tf_op jit(solution)/shard_map/all_to_all | solution.py:91
  155.2 3.3 %all-to-all-start.4 = ((f32[8,2,256]{2,1,0:T(2,128)}), f32[8,2,256]{2,1,0:T(2,128)S(1)}, u32[]{:S(2)}, u32[]{:S(2)}) async-start(f32[8,2,256]{2,1,0:T(2,128)} %broadcast_in_dim.17), calls=%async_computation.4 | async-start | bytes 32768 | tf_op jit(solution)/shard_map/all_to_all | solution.py:91
  158.6 1.7 fusion.37
  160.3 3.6 %all-to-all-done.4 = f32[8,2,256]{2,1,0:T(2,128)S(1)} async-done(((f32[8,2,256]{2,1,0:T(2,128)}), f32[8,2,256]{2,1,0:T(2,128)S(1)}, u32[]{:S(2)}, u32[]{:S(2)}) %all-to-all-start.4) | async-done | bytes 16416 | tf_op jit(solution)/shard_map/all_to_all | solution.py:91
  164.5 5.0 %all-to-all-start.5 = ((f32[32,2,256]{2,1,0:T(2,128)}), f32[32,2,256]{2,1,0:T(2,128)S(1)}, u32[]{:S(2)}, u32[]{:S(2)}) async-start(f32[32,2,256]{2,1,0:T(2,128)} %broadcast_in_dim.18), calls=%async_computation.5 | async-start | bytes 131072 | tf_op jit(solution)/shard_map/all_to_all | solution.py:91
  169.5 1.8 fusion.41
  171.3 7.2 %all-to-all-done.5 = f32[32,2,256]{2,1,0:T(2,128)S(1)} async-done(((f32[32,2,256]{2,1,0:T(2,128)}), f32[32,2,256]{2,1,0:T(2,128)S(1)}, u32[]{:S(2)}, u32[]{:S(2)}) %all-to-all-start.5) | async-done | bytes 65568 | tf_op jit(solution)/shard_map/all_to_all | solution.py:91
  179.1 6.9 %all-gather.6.cloned.1.call-done = bf16[2048,256]{1,0:T(8,128)(2,1)} async-done(((bf16[256,256]{1,0:T(8,128)(2,1)}), bf16[2048,256]{1,0:T(8,128)(2,1)}) %all-gather.6.cloned.1.call-update) | async-done | bytes 1048592 | tf_op jit(solution)/shard_map/all_gather | solution.py:161
  186.0 3.7 %convolution_convert_fusion = bf16[2048,256]{1,0:T(8,128)(2,1)S(1)} fusion(bf16[256,256]{1,0:T(8,128)(2,1)} %param.12, bf16[2048,256]{1,0:T(8,128)(2,1)S(1)} %bitcast.79, f32[2048,256]{1,0:T(8,128)} %fusion.41, bf16[2048,256]{1,0:T(8,128)(2,1)} %all-gather.6.cloned.1.call-done, f32[256]{0:T(256)S(1)} %bitcast.92, f32[256]{0:T(256)S(1)} %bitcast.89, ...), kind=kOutput, calls=%fused_computation.5 | convolution fusion | flops 547356672 | bytes 5381120 | tf_op jit(solution)/shard_map/ng,fg->nf/dot_general | solution.py:195
  189.7 13.8 %backward_edges.1 = (bf16[16,256,256]{2,1,0:T(8,128)(2,1)}, bf16[16,256,256]{2,1,0:T(8,128)(2,1)S(1)}) custom-call(s32[1]{0:T(128)} %bitcast.13.core_ref, bf16[8,256,256]{2,1,0:T(8,128)(2,1)S(1)} %bitcast.75, f32[32,8,256]{2,1,0:T(8,128)S(1)} %pad_convert_fusion.edge_ref), custom_call_target="tpu_custom_call" | custom-call | tf_op jit(solution)/shard_map/backward_edges/pallas_call | solution.py:200
  203.4 1.5 fusion.16
  205.3 30.9 %all_to_all.46 = f32[256,2,256]{2,1,0:T(2,128)S(1)} all-to-all(f32[256,2,256]{2,1,0:T(2,128)S(1)} %reshape.271), channel_id=1, replica_groups=mesh['x'=4,'c'=2,'y'=4,'z'=8] {'x','c','y','z'}, dimensions={0} | all-to-all | bytes 1048576 | tf_op jit(solution)/shard_map/all_to_all | solution.py:91
  236.5 0.9 broadcast_in_dim.19
  237.4 6.5 %all-to-all-start.8 = ((f32[256,2,256]{2,1,0:T(2,128)}), f32[256,2,256]{2,1,0:T(2,128)S(1)}, u32[]{:S(2)}, u32[]{:S(2)}) async-start(f32[256,2,256]{2,1,0:T(2,128)} %broadcast_in_dim.19), calls=%async_computation.8 | async-start | bytes 1048576 | tf_op jit(solution)/shard_map/all_to_all | solution.py:91
  243.9 3.6 %add_convert_fusion = bf16[16,256,256]{2,1,0:T(8,128)(2,1)} fusion(bf16[16,256,256]{2,1,0:T(8,128)(2,1)} %collective-permute-done, bf16[16,256,256]{2,1,0:T(8,128)(2,1)S(1)} %get-tuple-element.7), kind=kLoop, calls=%fused_computation.1 | loop fusion | flops 4194304 | bytes 6291456 | tf_op jit(solution)/shard_map/convert_element_type | solution.py:210
  247.4 16.9 %all-to-all-done.8 = f32[256,2,256]{2,1,0:T(2,128)S(1)} async-done(((f32[256,2,256]{2,1,0:T(2,128)}), f32[256,2,256]{2,1,0:T(2,128)S(1)}, u32[]{:S(2)}, u32[]{:S(2)}) %all-to-all-start.8) | async-done | bytes 524320 | tf_op jit(solution)/shard_map/all_to_all | solution.py:91
  264.3 4.9 %all-to-all-start.6 = ((bf16[16,256,256]{2,1,0:T(8,128)(2,1)}), bf16[16,256,256]{2,1,0:T(8,128)(2,1)S(1)}, u32[]{:S(2)}, u32[]{:S(2)}) async-start(bf16[16,256,256]{2,1,0:T(8,128)(2,1)} %add_convert_fusion), calls=%async_computation.6 | async-start | bytes 4194304 | tf_op jit(solution)/shard_map/all_to_all | solution.py:91
  269.5 0.9 slice.47
  270.4 0.9 slice.45
  271.3 30.1 %all-to-all-done.6 = bf16[16,256,256]{2,1,0:T(8,128)(2,1)S(1)} async-done(((bf16[16,256,256]{2,1,0:T(8,128)(2,1)}), bf16[16,256,256]{2,1,0:T(8,128)(2,1)S(1)}, u32[]{:S(2)}, u32[]{:S(2)}) %all-to-all-start.6) | async-done | bytes 2097184 | tf_op jit(solution)/shard_map/all_to_all | solution.py:91
  301.7 1.0 fusion.7
  (76 shorter events, 9.1 us)
Async XLA Ops:
  7.2 83.9 %copy-start = (bf16[256,256]{1,0:T(8,128)(2,1)S(1)}, bf16[256,256]{1,0:T(8,128)(2,1)}, u32[]{:S(2)}) copy-start(bf16[256,256]{1,0:T(8,128)(2,1)} %param.11) | copy-start | bytes 393220
  7.2 57.1 %all-gather.8.cloned.1.call-start = ((), (), s32[]{:S(2)}) async-start(), calls=%async_computation.10 | async-start | bytes 4325376 | tf_op jit(solution)/shard_map/all_gather | solution.py:128
  11.0 9.6 %all-to-all-start = ((bf16[4,32,256]{2,1,0:T(8,128)(2,1)}), bf16[4,32,256]{2,1,0:T(8,128)(2,1)S(1)}, u32[]{:S(2)}, u32[]{:S(2)}) async-start(bf16[4,32,256]{2,1,0:T(8,128)(2,1)} %reshape.267), calls=%async_computation | async-start | bytes 131072 | tf_op jit(solution)/shard_map/all_to_all | solution.py:91
  16.4 142.2 %all-gather.10.cloned.1.call-start = ((), (), s32[]{:S(2)}) async-start(), calls=%async_computation.11 | async-start | bytes 2359296 | tf_op jit(solution)/shard_map/all_gather | solution.py:131
  64.2 2.2 copy-start.1
  83.9 7.2 %copy-start.5 = (bf16[256,256]{1,0:T(8,128)(2,1)S(1)}, bf16[256,256]{1,0:T(8,128)(2,1)}, u32[]{:S(2)}) copy-start(bf16[256,256]{1,0:T(8,128)(2,1)} %param.10) | copy-start | bytes 393220
  83.9 42.9 %copy-start.8 = (bf16[256,256]{1,0:T(8,128)(2,1)S(1)}, bf16[256,256]{1,0:T(8,128)(2,1)}, u32[]{:S(2)}) copy-start(bf16[256,256]{1,0:T(8,128)(2,1)} %param.12) | copy-start | bytes 393220
  83.9 42.7 %all-to-all-start.1 = ((bf16[8,256,256]{2,1,0:T(8,128)(2,1)}), bf16[8,256,256]{2,1,0:T(8,128)(2,1)S(1)}, u32[]{:S(2)}, u32[]{:S(2)}) async-start(bf16[8,256,256]{2,1,0:T(8,128)(2,1)} %forward_edges.1), calls=%async_computation.1 | async-start | bytes 2097152 | tf_op jit(solution)/shard_map/all_to_all | solution.py:91
  91.1 62.7 %copy-start.9 = (f32[256]{0:T(256)S(1)}, f32[256]{0:T(256)}, u32[]{:S(2)}) copy-start(f32[256]{0:T(256)} %param.13) | copy-start | bytes 3076
  91.1 63.3 %copy-start.6 = (bf16[256,256]{1,0:T(8,128)(2,1)S(1)}, bf16[256,256]{1,0:T(8,128)(2,1)}, u32[]{:S(2)}) copy-start(bf16[256,256]{1,0:T(8,128)(2,1)} %param.15) | copy-start | bytes 393220
  91.1 63.3 %copy-start.10 = (f32[256]{0:T(256)S(1)}, f32[256]{0:T(256)}, u32[]{:S(2)}) copy-start(f32[256]{0:T(256)} %param.14) | copy-start | bytes 3076
  126.8 18.1 %copy-start.4 = (bf16[256,256]{1,0:T(8,128)(2,1)}, bf16[256,256]{1,0:T(8,128)(2,1)S(1)}, u32[]{:S(2)}) copy-start(bf16[256,256]{1,0:T(8,128)(2,1)S(1)} %reduce_sum.138) | copy-start | bytes 393220
  127.0 31.6 %copy-start.2 = (f32[256,256]{1,0:T(8,128)}, f32[256,256]{1,0:T(8,128)S(1)}, u32[]{:S(2)}) copy-start(f32[256,256]{1,0:T(8,128)S(1)} %get-tuple-element.30) | copy-start | bytes 786436
  137.0 16.7 %all-to-all-start.3 = ((f32[32,2,256]{2,1,0:T(2,128)}), f32[32,2,256]{2,1,0:T(2,128)S(1)}, u32[]{:S(2)}, u32[]{:S(2)}) async-start(f32[32,2,256]{2,1,0:T(2,128)} %broadcast_in_dim.16), calls=%async_computation.3 | async-start | bytes 131072 | tf_op jit(solution)/shard_map/all_to_all | solution.py:91
  144.9 41.1 %all-gather.6.cloned.1.call-start = ((), (), s32[]{:S(2)}) async-start(), calls=%async_computation.9 | async-start | bytes 1179648 | tf_op jit(solution)/shard_map/all_gather | solution.py:161
  155.2 8.6 %all-to-all-start.4 = ((f32[8,2,256]{2,1,0:T(2,128)}), f32[8,2,256]{2,1,0:T(2,128)S(1)}, u32[]{:S(2)}, u32[]{:S(2)}) async-start(f32[8,2,256]{2,1,0:T(2,128)} %broadcast_in_dim.17), calls=%async_computation.4 | async-start | bytes 32768 | tf_op jit(solution)/shard_map/all_to_all | solution.py:91
  164.5 14.0 %all-to-all-start.5 = ((f32[32,2,256]{2,1,0:T(2,128)}), f32[32,2,256]{2,1,0:T(2,128)S(1)}, u32[]{:S(2)}, u32[]{:S(2)}) async-start(f32[32,2,256]{2,1,0:T(2,128)} %broadcast_in_dim.18), calls=%async_computation.5 | async-start | bytes 131072 | tf_op jit(solution)/shard_map/all_to_all | solution.py:91
  179.1 10.6 %copy-start.12 = (f32[1,256]{1,0:T(1,128)}, f32[1,256]{1,0:T(1,128)S(1)}, u32[]{:S(2)}) copy-start(f32[1,256]{1,0:T(1,128)S(1)} %get-tuple-element.26) | copy-start | bytes 3076
  179.1 10.6 %copy-start.14 = (f32[1,256]{1,0:T(1,128)}, f32[1,256]{1,0:T(1,128)S(1)}, u32[]{:S(2)}) copy-start(f32[1,256]{1,0:T(1,128)S(1)} %get-tuple-element.27) | copy-start | bytes 3076
  203.4 40.4 %collective-permute-start = (bf16[16,256,256]{2,1,0:T(8,128)(2,1)}, bf16[16,256,256]{2,1,0:T(8,128)(2,1)}, u32[]{:S(2)}, u32[]{:S(2)}) collective-permute-start(bf16[16,256,256]{2,1,0:T(8,128)(2,1)} %get-tuple-element.8), channel_id=1, source_target_pairs={{0,32},{32,0},{1,33},{33,1},{2,34},{34,2},{3,35},{35,3},{4,36},{36... | collective-permute-start | bytes 6291464 | tf_op jit(solution)/shard_map/ppermute | solution.py:209
  237.4 26.9 %all-to-all-start.8 = ((f32[256,2,256]{2,1,0:T(2,128)}), f32[256,2,256]{2,1,0:T(2,128)S(1)}, u32[]{:S(2)}, u32[]{:S(2)}) async-start(f32[256,2,256]{2,1,0:T(2,128)} %broadcast_in_dim.19), calls=%async_computation.8 | async-start | bytes 1048576 | tf_op jit(solution)/shard_map/all_to_all | solution.py:91
  264.3 37.1 %all-to-all-start.6 = ((bf16[16,256,256]{2,1,0:T(8,128)(2,1)}), bf16[16,256,256]{2,1,0:T(8,128)(2,1)S(1)}, u32[]{:S(2)}, u32[]{:S(2)}) async-start(bf16[16,256,256]{2,1,0:T(8,128)(2,1)} %add_convert_fusion), calls=%async_computation.6 | async-start | bytes 4194304 | tf_op jit(solution)/shard_map/all_to_all | solution.py:91
  269.3 32.4 %copy-start.3 = (f32[256,256]{1,0:T(8,128)S(1)}, f32[256,256]{1,0:T(8,128)}, u32[]{:S(2)}) copy-start(f32[256,256]{1,0:T(8,128)} %copy-done.2) | copy-start | bytes 786436
  269.5 32.2 %copy-start.7 = (bf16[256,256]{1,0:T(8,128)(2,1)S(1)}, bf16[256,256]{1,0:T(8,128)(2,1)}, u32[]{:S(2)}) copy-start(bf16[256,256]{1,0:T(8,128)(2,1)} %param.15) | copy-start | bytes 393220
  269.5 32.2 %copy-start.11 = (f32[256]{0:T(256)S(1)}, f32[256]{0:T(256)}, u32[]{:S(2)}) copy-start(f32[256]{0:T(256)} %get-tuple-element.15) | copy-start | bytes 3076
  269.5 32.2 %copy-start.13 = (f32[1,256]{1,0:T(1,128)S(1)}, f32[1,256]{1,0:T(1,128)}, u32[]{:S(2)}) copy-start(f32[1,256]{1,0:T(1,128)} %copy-done.12) | copy-start | bytes 3076
  269.5 32.2 %copy-start.15 = (f32[1,256]{1,0:T(1,128)S(1)}, f32[1,256]{1,0:T(1,128)}, u32[]{:S(2)}) copy-start(f32[1,256]{1,0:T(1,128)} %copy-done.14) | copy-start | bytes 3076
Sparse Core Ops, SparseCore 0:
  10.6 53.6 all-gather.7
  66.6 58.3 all-gather.9
  148.1 37.8 all-gather.5
